TPU v7x, 32 devices: a whole 2x2x4 slice. The times are simulated.
32 devices in a mesh: grp: 2 (over x), tmpl: 16 (over z, y, core).
Axes of the slice: x: 2, y: 2, z: 4, core: 2. Of those that a mesh axis runs over, the one named last changes fastest.
Arguments:
- strain: float32 [16, 512, 1024], P('grp', None, 'tmpl'), parts along dimension 0, may hold values from -6 to 6
- analysis: float32 [1024, 1024], P('grp', 'tmpl'), parts along dimension 0, may hold values from -6 to 6
- bank: bfloat16 [2, 16, 512, 512], P(None, None, 'tmpl'), may hold values from -6 to 6
- cutoff: int32 [16], replicated, may hold values from 65536 to 262144
- order: int32 [16], replicated, may hold values from 0 to 15, each once
Outputs:
- snr: bfloat16 [32, 512, 1024], P(('grp', 'tmpl')), parts along dimension 0
There are 2 independent parts, one for each index of `grp`. A program takes and returns all parts, laid end to end along the dimension named above; an argument that names none is the same for every part. Nothing has to cross between parts.
Inputs may be any that keep to these rules, and one draw needn't show every extreme that they name: `order`: a permutation of the bank's templates.
All inputs are finite; a program needn't handle non-finite values.
Results may differ from a plain program's by a relative error of at most 0.013.
Values may be sent and summed in bfloat16 or wider, within the bound.
A program may use at most 64 MiB of HBM per device.

v0:
```python
import functools
import math

import jax
import jax.numpy as jnp
import numpy as np
from jax import lax
from jax.experimental import pallas as pl
from jax.experimental.pallas import tpu as pltpu
from jax.sharding import PartitionSpec as P


def angles(left_idx, right_idx, period):
    product = left_idx[:, None] * right_idx[None, :] % period
    phase_angle = product.astype(jnp.float32) * (2.0 * math.pi / period)
    return (jnp.cos(phase_angle), jnp.sin(phase_angle))


def filtered(white_pair, tmpl_pair, cut_bins, freq_bin):
    white_real = white_pair[0].astype(jnp.float32)
    white_imag = white_pair[1].astype(jnp.float32)
    tmpl_real = tmpl_pair[0].astype(jnp.float32)
    tmpl_imag = tmpl_pair[1].astype(jnp.float32)
    in_band = freq_bin[None] < cut_bins[:, None, None]
    filt_real = jnp.where(in_band, white_real * tmpl_real + white_imag * tmpl_imag, 0.0)
    filt_imag = jnp.where(in_band, white_imag * tmpl_real - white_real * tmpl_imag, 0.0)
    return jnp.concatenate([filt_real, filt_imag], -1).astype(jnp.bfloat16)


def inverse_rows(stacked, row_bins, second_len, length):
    half_len = second_len // 2
    cosine, sine = angles(
        jnp.arange(half_len, dtype=jnp.int32), jnp.arange(second_len, dtype=jnp.int32), second_len
    )
    dft_table = jnp.concatenate(
        [jnp.concatenate([cosine, sine], 1), jnp.concatenate([-sine, cosine], 1)], 0
    ).astype(jnp.bfloat16)
    spread = jnp.einsum("tkf,fg->tkg", stacked, dft_table, preferred_element_type=jnp.float32)
    spread_real = spread[..., :second_len]
    spread_imag = spread[..., second_len:]
    cos_twist, sin_twist = angles(row_bins, jnp.arange(second_len, dtype=jnp.int32), length)
    lift_real = spread_real * cos_twist - spread_imag * sin_twist
    lift_imag = spread_real * sin_twist + spread_imag * cos_twist
    return jnp.concatenate([lift_real, lift_imag], -1).astype(jnp.bfloat16)


def inverse_cols(lifted, first_len, second_len):
    row_idx = jnp.arange(first_len, dtype=jnp.int32)
    cosine, sine = angles(row_idx, row_idx, first_len)
    cosine = cosine.astype(jnp.bfloat16)
    sine = sine.astype(jnp.bfloat16)
    lift_real = lifted[..., :second_len]
    lift_imag = lifted[..., second_len:]
    field_real = jnp.einsum(
        "ak,tkb->tab", cosine, lift_real, preferred_element_type=jnp.float32
    ) - jnp.einsum("ak,tkb->tab", sine, lift_imag, preferred_element_type=jnp.float32)
    field_imag = jnp.einsum(
        "ak,tkb->tab", sine, lift_real, preferred_element_type=jnp.float32
    ) + jnp.einsum("ak,tkb->tab", cosine, lift_imag, preferred_element_type=jnp.float32)
    return (field_real, field_imag)


def local(strain, analysis, bank, cutoff, order):
    highest = lax.Precision.HIGHEST
    dev_count = lax.axis_size("tmpl")
    my_index = lax.axis_index("tmpl")
    seg_count = strain.shape[0]
    first_len = strain.shape[1]
    col_count = strain.shape[2]
    second_len = col_count * dev_count
    length = first_len * second_len
    half_len = second_len // 2
    row_count = first_len // dev_count
    row_idx = jnp.arange(first_len, dtype=jnp.int32)
    col_index = my_index * col_count + jnp.arange(col_count, dtype=jnp.int32)
    sample_idx = row_idx[:, None] * second_len + col_index[None, :]
    window = (
        math.sqrt(8.0 / 3.0) * jnp.sin(sample_idx.astype(jnp.float32) * (math.pi / length)) ** 2
    )
    series = jnp.concatenate([strain * window, analysis[None]], 0)
    cos_one, sin_one = angles(row_idx, row_idx, first_len)
    part_real = jnp.einsum("ka,sab->skb", cos_one, series, precision=highest)
    part_imag = -jnp.einsum("ka,sab->skb", sin_one, series, precision=highest)
    cos_twist, sin_twist = angles(row_idx, col_index, length)
    twist_real = part_real * cos_twist + part_imag * sin_twist
    twist_imag = part_imag * cos_twist - part_real * sin_twist
    moved = lax.all_to_all(
        jnp.stack([twist_real, twist_imag]).astype(jnp.bfloat16),
        "tmpl",
        split_axis=2,
        concat_axis=3,
        tiled=True,
    ).astype(jnp.float32)
    cos_two, sin_two = angles(
        jnp.arange(second_len, dtype=jnp.int32), jnp.arange(half_len, dtype=jnp.int32), second_len
    )
    spec_real = jnp.einsum("skb,bf->skf", moved[0], cos_two, precision=highest) + jnp.einsum(
        "skb,bf->skf", moved[1], sin_two, precision=highest
    )
    spec_imag = jnp.einsum("skb,bf->skf", moved[1], cos_two, precision=highest) - jnp.einsum(
        "skb,bf->skf", moved[0], sin_two, precision=highest
    )
    power_spec = jnp.maximum(
        jnp.mean(spec_real[:seg_count] ** 2 + spec_imag[:seg_count] ** 2, axis=0), 0.2 * length
    )
    whitened = jnp.stack(
        [spec_real[seg_count] / power_spec, spec_imag[seg_count] / power_spec]
    ).astype(jnp.bfloat16)
    own_rows = my_index * row_count + jnp.arange(row_count, dtype=jnp.int32)
    half_idx = jnp.arange(half_len, dtype=jnp.int32)
    freq_local = own_rows[:, None] + first_len * half_idx[None, :]
    pick = (order[:, None] == jnp.arange(order.shape[0], dtype=jnp.int32)[None, :]).astype(bank.dtype)
    chosen = jnp.einsum("jt,ctkf->cjkf", pick, bank)
    cuts = jnp.take(cutoff, order)
    bank_real = chosen[0].astype(jnp.float32)
    bank_imag = chosen[1].astype(jnp.float32)
    in_band = freq_local[None] < cuts[:, None, None]
    local_norm = jnp.sum(
        jnp.where(in_band, (bank_real**2 + bank_imag**2) / power_spec, 0.0), axis=(1, 2)
    )
    norm_sq = lax.psum(local_norm, "tmpl")
    per_device = cuts.shape[0] // dev_count
    own_norm = lax.dynamic_slice_in_dim(norm_sq, my_index * per_device, per_device)
    stacked = filtered(whitened, chosen, cuts, freq_local)
    lifted = lax.all_to_all(
        inverse_rows(stacked, own_rows, second_len, length),
        "tmpl",
        split_axis=0,
        concat_axis=1,
        tiled=True,
    )
    field_real, field_imag = inverse_cols(lifted, first_len, second_len)
    magnitude = jnp.sqrt(field_real**2 + field_imag**2)
    return (magnitude / jnp.sqrt(own_norm)[:, None, None]).astype(jnp.bfloat16)


def unit(left, right, period):
    phase = (left[:, None] * right[None, :] % period) * (2.0 * np.pi / period)
    return np.cos(phase), np.sin(phase)


def tables(devs, first, cols):
    second = cols * devs
    half = second // 2
    length = first * second
    rows = first // devs
    k1 = np.arange(first, dtype=np.int64)
    b = np.arange(second, dtype=np.int64)
    cos, sin = unit(k1, k1, first)
    fwd_one = np.stack([cos.reshape(devs, rows, first), sin.reshape(devs, rows, first)], 1)
    fwd_one = fwd_one.reshape(devs, 2 * rows, first)
    samples = k1[:, None] * second + b[None, :]
    window = np.sqrt(8.0 / 3.0) * np.sin(samples * (np.pi / length)) ** 2
    tcos, tsin = unit(k1, b, length)

    def paired(left, right):
        split = [part.reshape(first, devs, cols).transpose(1, 0, 2) for part in (left, right)]
        return np.concatenate(split, 2)

    window = paired(window, window)
    twist_cos = paired(tcos, tcos)
    twist_sin = paired(tsin, -tsin)
    low = np.arange(half, dtype=np.int64)
    blocks = []
    for bins in (low, second - 1 - low):
        cos, sin = unit(b, bins, second)
        real = np.concatenate([cos.reshape(devs, cols, half), sin.reshape(devs, cols, half)], 1)
        imag = np.concatenate([-sin.reshape(devs, cols, half), cos.reshape(devs, cols, half)], 1)
        blocks += [real.reshape(2 * second, half), imag.reshape(2 * second, half)]
    fwd_two = np.concatenate(blocks, 1)
    cos, sin = unit(low, b, second)
    inv_one = np.block([[cos, sin], [-sin, cos]])
    cos, sin = unit(k1, k1, first)
    inv_two = np.block([[cos, -sin], [sin, cos]])
    found = (fwd_one, window, twist_cos, twist_sin, fwd_two, inv_one, tcos, tsin, inv_two)
    return [part.astype(np.float32).astype(jnp.bfloat16) for part in found]


def kernel(
    devs, group,
    cutoff, order, strain_h, analysis_h, bank_h, one_h, window_h, tcos_h, tsin_h, two_h, inv_h, ucos_h, usin_h, last_h,
    out,
    strain, analysis, bank, one, window, tcos, tsin, two, inv, ucos, usin, last,
    series, send_a, recv_a, spec, mirror_out, mirror_in, edge_out, edge_in, send_q, recv_q, norm_out, norm_in, lifted,
    load_sem, a_send, a_recv, m_send, m_recv, q_send, q_recv, n_send, n_recv,
):
    f32, bf16 = jnp.float32, jnp.bfloat16
    me = lax.axis_index("tmpl")
    segs, first, cols = strain.shape
    pairs = segs // 2
    width = 2 * cols
    rows = first // devs
    second = cols * devs
    half = second // 2
    length = first * second
    packed = pairs * rows

    loads = []
    for at, (src, dst) in enumerate([
        (strain_h, strain), (analysis_h, analysis), (window_h.at[me], window), (one_h, one),
        (tcos_h.at[me], tcos), (tsin_h.at[me], tsin), (two_h, two), (bank_h, bank),
        (inv_h, inv), (ucos_h, ucos), (usin_h, usin), (last_h, last),
    ]):
        copy = pltpu.make_async_copy(src, dst, load_sem.at[at])
        copy.start()
        loads.append(copy)

    barrier = pltpu.get_barrier_semaphore()

    def greet(step, carry):
        pl.semaphore_signal(barrier, inc=1, device_id={"tmpl": lax.rem(me + step, devs)},
                            device_id_type=pl.DeviceIdType.MESH)
        return carry

    lax.fori_loop(1, devs, greet, 0)

    for copy in loads[:6]:
        copy.wait()
    for pair in range(pairs):
        both = jnp.concatenate([strain[2 * pair], strain[2 * pair + 1]], 1)
        series[:, pair * width:(pair + 1) * width] = (both * window[...].astype(f32)).astype(bf16)
    series[:, pairs * width:] = jnp.concatenate(
        [analysis[...], jnp.zeros((first, cols), f32)], 1).astype(bf16)
    lane = lax.broadcasted_iota(jnp.int32, (rows, width), 1)
    sign = jnp.where(lane < cols, -1.0, 1.0)

    pl.semaphore_wait(barrier, devs - 1)

    def a_copy(peer, source):
        return pltpu.make_async_remote_copy(
            src_ref=send_a.at[peer],
            dst_ref=recv_a.at[:, pl.ds(pl.multiple_of(source * width, width), width)],
            send_sem=a_send.at[peer], recv_sem=a_recv.at[source],
            device_id={"tmpl": peer}, device_id_type=pl.DeviceIdType.MESH)

    own_set = me // group
    sets = devs // group

    def spread(step, carry):
        chunk = lax.rem(own_set + 1 + step, sets)
        part = jnp.dot(one[pl.ds(chunk * group, group)].reshape(group * 2 * rows, first), series[...],
                       preferred_element_type=f32)
        for member in range(group):
            peer = chunk * group + member
            at = pl.ds(pl.multiple_of(peer * rows, rows), rows)
            cos, sin = tcos[at, :].astype(f32), tsin[at, :].astype(f32)
            base = member * 2 * rows
            for seg in range(pairs + 1):
                upper = part[base:base + rows, seg * width:(seg + 1) * width]
                lower = part[base + rows:base + 2 * rows, seg * width:(seg + 1) * width]
                field = upper + pltpu.roll(lower * sign, cols, 1)
                field = field * cos + pltpu.roll(field, cols, 1) * sin
                send_a[peer, seg * rows:(seg + 1) * rows, :] = field.astype(bf16)

            @pl.when(peer != me)
            def _():
                a_copy(peer, me).start()
        return carry

    lax.fori_loop(0, sets, spread, 0)
    recv_a[:, pl.ds(pl.multiple_of(me * width, width), width)] = send_a[me]
    loads[6].wait()

    def others(body):
        def step(at, carry):
            body(lax.rem(me + at, devs))
            return carry
        lax.fori_loop(1, devs, step, 0)

    others(lambda peer: a_copy(peer, peer).wait_recv())

    chunk_cols = min(half, 512)

    def columns(step, carry):
        at = pl.ds(pl.multiple_of(step * chunk_cols, chunk_cols), chunk_cols)
        spec[:, at] = jnp.dot(recv_a[...], two[:, at], preferred_element_type=f32)
        return carry

    lax.fori_loop(0, 2 * second // chunk_cols, columns, 0)

    def power(start):
        total = jnp.zeros((rows, half), f32)
        for pair in range(pairs):
            for part in (start, start + half):
                value = spec[pair * rows:(pair + 1) * rows, part:part + half]
                total = total + value * value
        return total

    far = power(second)
    near_row = lax.broadcasted_iota(jnp.int32, (rows, rows), 0)
    near_col = lax.broadcasted_iota(jnp.int32, (rows, rows), 1)
    flip = jnp.where(near_row + near_col == rows, 1.0, 0.0)
    mirror_out[...] = jnp.dot(flip, far, preferred_element_type=f32, precision=lax.Precision.HIGHEST)
    edge_out[...] = far[:8]
    partner = devs - 1 - me
    edge_partner = lax.rem(devs - me, devs)
    mirror_copy = pltpu.make_async_remote_copy(
        src_ref=mirror_out, dst_ref=mirror_in, send_sem=m_send.at[0], recv_sem=m_recv.at[0],
        device_id={"tmpl": partner}, device_id_type=pl.DeviceIdType.MESH)
    edge_copy = pltpu.make_async_remote_copy(
        src_ref=edge_out, dst_ref=edge_in, send_sem=m_send.at[1], recv_sem=m_recv.at[1],
        device_id={"tmpl": edge_partner}, device_id_type=pl.DeviceIdType.MESH)
    mirror_copy.start()

    @pl.when(edge_partner != me)
    def _():
        edge_copy.start()
    close = power(0)

    @pl.when(edge_partner == me)
    def _():
        edge_lane = lax.broadcasted_iota(jnp.int32, (8, half), 1)
        shifted = jnp.where(edge_lane == 0, close[:8], pltpu.roll(far[:8], 1, 1))
        edge_in[...] = jnp.where(me == 0, shifted, far[:8])

    @pl.when(edge_partner != me)
    def _():
        edge_copy.wait_recv()
    mirror_copy.wait_recv()
    row = lax.broadcasted_iota(jnp.int32, (rows, half), 0)
    opposite = jnp.where(row == 0, edge_in[0:1, :], mirror_in[...])
    inverse = 1.0 / jnp.maximum((close + opposite) * (0.5 / segs), 0.2 * length)
    white_real = (spec[packed:, :half] * inverse).astype(bf16).astype(f32)
    white_imag = (spec[packed:, half:second] * inverse).astype(bf16).astype(f32)
    freq = me * rows + row + first * lax.broadcasted_iota(jnp.int32, (rows, half), 1)
    loads[7].wait()

    def q_copy(peer, source):
        return pltpu.make_async_remote_copy(
            src_ref=send_q.at[peer],
            dst_ref=recv_q.at[pl.ds(pl.multiple_of(source * rows, rows), rows), :],
            send_sem=q_send.at[peer], recv_sem=q_recv.at[source],
            device_id={"tmpl": peer}, device_id_type=pl.DeviceIdType.MESH)

    def n_copy(peer, source):
        return pltpu.make_async_remote_copy(
            src_ref=norm_out.at[peer], dst_ref=norm_in.at[source],
            send_sem=n_send.at[peer], recv_sem=n_recv.at[source],
            device_id={"tmpl": peer}, device_id_type=pl.DeviceIdType.MESH)

    def filters(step, carry):
        peer = lax.rem(me + step, devs)
        which = order[peer]
        inside = freq < cutoff[which]
        real, imag = bank[0, which].astype(f32), bank[1, which].astype(f32)
        send_q[peer, :, :half] = jnp.where(inside, white_real * real + white_imag * imag, 0.0).astype(bf16)
        send_q[peer, :, half:] = jnp.where(inside, white_imag * real - white_real * imag, 0.0).astype(bf16)
        weight = jnp.where(inside, (real * real + imag * imag) * inverse, 0.0)
        total = sum(weight[at:at + 8] for at in range(0, rows, 8))
        norm_out[peer] = sum(total[:, at:at + 128] for at in range(0, half, 128))

        @pl.when(peer != me)
        def _():
            q_copy(peer, me).start()
            n_copy(peer, me).start()
        return carry

    lax.fori_loop(1, devs + 1, filters, 0)
    recv_q[pl.ds(pl.multiple_of(me * rows, rows), rows), :] = send_q[me]
    norm_in[me] = norm_out[me]
    for copy in loads[8:]:
        copy.wait()

    def rows_back(step, carry):
        chunk = lax.rem(own_set + step, sets)
        for member in range(group):
            peer = chunk * group + member

            @pl.when(peer != me)
            def _():
                q_copy(peer, peer).wait_recv()
        at = pl.ds(pl.multiple_of(chunk * group * rows, group * rows), group * rows)
        below = pl.ds(pl.multiple_of(first + chunk * group * rows, group * rows), group * rows)
        wide = jnp.dot(recv_q[at, :], inv[...], preferred_element_type=f32)
        real, imag = wide[:, :second], wide[:, second:]
        cos, sin = ucos[at, :].astype(f32), usin[at, :].astype(f32)
        lifted[at, :] = (real * cos - imag * sin).astype(bf16)
        lifted[below, :] = (real * sin + imag * cos).astype(bf16)
        return carry

    lax.fori_loop(0, sets, rows_back, 0)
    others(lambda peer: n_copy(peer, peer).wait_recv())
    norm = jnp.sum(jnp.sum(jnp.sum(norm_in[...], 0), 0, keepdims=True), 1, keepdims=True)
    gain = 1.0 / jnp.sqrt(norm)
    tail = 256

    def cols_back(step, carry):
        at = pl.ds(pl.multiple_of(step * tail, tail), tail)
        field = jnp.dot(last[...], lifted[:, at], preferred_element_type=f32)
        real, imag = field[:first], field[first:]
        out[0, :, at] = (jnp.sqrt(real * real + imag * imag) * gain).astype(bf16)
        return carry

    lax.fori_loop(0, second // tail, cols_back, 0)

    def drain(peer):
        a_copy(peer, me).wait_send()
        q_copy(peer, me).wait_send()
        n_copy(peer, me).wait_send()

    others(drain)
    mirror_copy.wait_send()

    @pl.when(edge_partner != me)
    def _():
        edge_copy.wait_send()


def fused(strain, analysis, bank, cutoff, order):
    devs = lax.axis_size("tmpl")
    segs, first, cols = strain.shape
    second = cols * devs
    half = second // 2
    rows = first // devs
    group = 4
    parts = segs // 2 + 1
    f32, bf16 = jnp.float32, jnp.bfloat16
    consts = [jnp.asarray(part) for part in tables(devs, first, cols)]
    smem = pl.BlockSpec(memory_space=pltpu.SMEM)
    held = [strain, analysis, bank] + consts
    shapes = [part.shape for part in held]
    for at in (4, 5, 6):
        shapes[at] = shapes[at][1:]
    vmem = pltpu.VMEM
    dma = pltpu.SemaphoreType.DMA
    return pl.pallas_call(
        functools.partial(kernel, devs, group),
        out_shape=jax.ShapeDtypeStruct((1, first, second), bf16),
        in_specs=[smem, smem] + [pl.BlockSpec(memory_space=pl.ANY)] * len(held),
        out_specs=pl.BlockSpec(memory_space=vmem),
        scratch_shapes=[vmem(shape, part.dtype) for shape, part in zip(shapes, held)] + [
            vmem((first, parts * 2 * cols), bf16),
            vmem((devs, parts * rows, 2 * cols), bf16),
            vmem((parts * rows, 2 * second), bf16),
            vmem((parts * rows, 2 * second), f32),
            vmem((rows, half), f32), vmem((rows, half), f32),
            vmem((8, half), f32), vmem((8, half), f32),
            vmem((devs, rows, 2 * half), bf16), vmem((first, 2 * half), bf16),
            vmem((devs, 8, 128), f32), vmem((devs, 8, 128), f32),
            vmem((2 * first, second), bf16),
            dma((len(held),)), dma((devs,)), dma((devs,)), dma((2,)), dma((2,)),
            dma((devs,)), dma((devs,)), dma((devs,)), dma((devs,)),
        ],
        compiler_params=pltpu.CompilerParams(
            collective_id=0, has_side_effects=True, vmem_limit_bytes=56 * 1024 * 1024),
    )(cutoff, order, *held)


def fits(strain, bank, devs):
    segs, first, cols = strain.shape
    rows = first // devs
    return (2 * cols == 128 and rows % 16 == 0 and segs % 2 == 0 and devs % 4 == 0
            and bank.shape[1] == devs)


def program(strain, analysis, bank, cutoff, order):
    if fits(strain, bank, lax.axis_size("tmpl")):
        return fused(strain, analysis, bank, cutoff, order)
    return local(strain, analysis, bank, cutoff, order)


def solution(mesh):
    return jax.shard_map(
        program,
        mesh=mesh,
        in_specs=(P("grp", None, "tmpl"), P("grp", "tmpl"), P(None, None, "tmpl", None), P(), P()),
        out_specs=P(("grp", "tmpl"), None, None),
        check_vma=False,
    )
```

profile of v0, /device:TPU:15, one launch (start us, length us, event | category | flops | bytes accessed | tf_op | source)
XLA Modules:
  0.0 66.9 jit_solution(2177794689490614904)
XLA Ops:
  0.0 1.7 %copy.16.analysis_h = f32[512,64]{1,0:T(8,128)} copy(f32[512,64]{0,1:T(8,128)} %param.15) | data formatting | bytes 262144 | tf_op args[1]
  1.7 3.2 %copy.15.strain_h = f32[8,512,64]{2,1,0:T(8,128)} copy(f32[8,512,64]{1,2,0:T(8,128)} %param.14) | data formatting | bytes 2097152 | tf_op args[0]
  4.9 59.7 %shard_map.136 = bf16[1,512,1024]{2,1,0:T(8,128)(2,1)} custom-call(s32[16]{0:T(128)} %cutoff.1, s32[16]{0:T(128)} %order.1, f32[8,512,64]{2,1,0:T(8,128)} %copy.15.strain_h, f32[512,64]{1,0:T(8,128)} %copy.16.analysis_h, bf16[2,16,32,512]{3,2,1,0:T(8,128)(2,1)} %bank_h.1, bf16[16,64,512]{2,1,0:T(8,128)(2,1)} %constant.18.clone.one_h, ...), custom_call_target="tpu_custom_call" | custom-call | tf_op jit(solution)/shard_map/pallas_call | solution.py:426
  64.7 2.3 %copy.18 = bf16[1,512,1024]{2,1,0:T(8,128)(2,1)} copy(bf16[1,512,1024]{2,1,0:T(8,128)(2,1)} %shard_map.136) | data formatting | bytes 2097152
where the time goes:
time: 67.1 us; the launch traced here: 66.9 us
  Pallas kernels  59.7 us (89%)
  local copies, waits for them, and re-layouts  7.19 us (11%)
    pallas_call x1, Pallas kernels, fused(): pl.pallas_call(functools.partial(kernel, devs, group), out_shape=jax.Shap...  59.7 us
    unnamed x3, local copies, waits for them, and re-layouts  7.19 us

commit v1 on v0

--- a/solution.py
+++ b/solution.py
@@ -134,6 +134,9 @@
     return (magnitude / jnp.sqrt(own_norm)[:, None, None]).astype(jnp.bfloat16)
 
 
+GROUP = 4
+
+
 def unit(left, right, period):
     phase = (left[:, None] * right[None, :] % period) * (2.0 * np.pi / period)
     return np.cos(phase), np.sin(phase)
@@ -157,7 +160,7 @@
         split = [part.reshape(first, devs, cols).transpose(1, 0, 2) for part in (left, right)]
         return np.concatenate(split, 2)
 
-    window = paired(window, window)
+    window = window.reshape(first, devs, cols).transpose(1, 2, 0)
     twist_cos = paired(tcos, tcos)
     twist_sin = paired(tsin, -tsin)
     low = np.arange(half, dtype=np.int64)
@@ -171,7 +174,8 @@
     cos, sin = unit(low, b, second)
     inv_one = np.block([[cos, sin], [-sin, cos]])
     cos, sin = unit(k1, k1, first)
-    inv_two = np.block([[cos, -sin], [sin, cos]])
+    inv_two = np.block([[cos, -sin], [sin, cos]]).reshape(2 * first, 2, devs // GROUP, GROUP * rows)
+    inv_two = inv_two.transpose(2, 0, 1, 3).reshape(devs // GROUP, 2 * first, 2 * GROUP * rows)
     found = (fwd_one, window, twist_cos, twist_sin, fwd_two, inv_one, tcos, tsin, inv_two)
     return [part.astype(np.float32).astype(jnp.bfloat16) for part in found]
 
@@ -181,12 +185,12 @@
     cutoff, order, strain_h, analysis_h, bank_h, one_h, window_h, tcos_h, tsin_h, two_h, inv_h, ucos_h, usin_h, last_h,
     out,
     strain, analysis, bank, one, window, tcos, tsin, two, inv, ucos, usin, last,
-    series, send_a, recv_a, spec, mirror_out, mirror_in, edge_out, edge_in, send_q, recv_q, norm_out, norm_in, lifted,
+    series, send_a, recv_a, spec, mirror_out, mirror_in, edge_out, edge_in, send_q, recv_q, norm_out, norm_in, lifted, total,
     load_sem, a_send, a_recv, m_send, m_recv, q_send, q_recv, n_send, n_recv,
 ):
     f32, bf16 = jnp.float32, jnp.bfloat16
     me = lax.axis_index("tmpl")
-    segs, first, cols = strain.shape
+    segs, cols, first = strain.shape
     pairs = segs // 2
     width = 2 * cols
     rows = first // devs
@@ -201,9 +205,9 @@
         (tcos_h.at[me], tcos), (tsin_h.at[me], tsin), (two_h, two), (bank_h, bank),
         (inv_h, inv), (ucos_h, ucos), (usin_h, usin), (last_h, last),
     ]):
-        copy = pltpu.make_async_copy(src, dst, load_sem.at[at])
+        loads.append(pltpu.make_async_copy(src, dst, load_sem.at[at]))
+    for copy in loads[:6]:
         copy.start()
-        loads.append(copy)
 
     barrier = pltpu.get_barrier_semaphore()
 
@@ -214,13 +218,16 @@
 
     lax.fori_loop(1, devs, greet, 0)
 
-    for copy in loads[:6]:
+    for copy in loads[:3]:
         copy.wait()
-    for pair in range(pairs):
-        both = jnp.concatenate([strain[2 * pair], strain[2 * pair + 1]], 1)
-        series[:, pair * width:(pair + 1) * width] = (both * window[...].astype(f32)).astype(bf16)
-    series[:, pairs * width:] = jnp.concatenate(
-        [analysis[...], jnp.zeros((first, cols), f32)], 1).astype(bf16)
+    for seg in range(segs):
+        series[seg * cols:(seg + 1) * cols, :] = (strain[seg] * window[...].astype(f32)).astype(bf16)
+    series[segs * cols:(segs + 1) * cols, :] = analysis[...].astype(bf16)
+    series[(segs + 1) * cols:, :] = jnp.zeros((cols, first), bf16)
+    for copy in loads[3:6]:
+        copy.wait()
+    for copy in loads[6:]:
+        copy.start()
     lane = lax.broadcasted_iota(jnp.int32, (rows, width), 1)
     sign = jnp.where(lane < cols, -1.0, 1.0)
 
@@ -238,8 +245,8 @@
 
     def spread(step, carry):
         chunk = lax.rem(own_set + 1 + step, sets)
-        part = jnp.dot(one[pl.ds(chunk * group, group)].reshape(group * 2 * rows, first), series[...],
-                       preferred_element_type=f32)
+        part = lax.dot_general(one[pl.ds(chunk * group, group)].reshape(group * 2 * rows, first), series[...],
+                               (((1,), (1,)), ((), ())), preferred_element_type=f32)
         for member in range(group):
             peer = chunk * group + member
             at = pl.ds(pl.multiple_of(peer * rows, rows), rows)
@@ -260,6 +267,8 @@
     lax.fori_loop(0, sets, spread, 0)
     recv_a[:, pl.ds(pl.multiple_of(me * width, width), width)] = send_a[me]
     loads[6].wait()
+    spec[...] = jnp.zeros(spec.shape, f32)
+    total[...] = jnp.zeros(total.shape, f32)
 
     def others(body):
         def step(at, carry):
@@ -267,24 +276,35 @@
             return carry
         lax.fori_loop(1, devs, step, 0)
 
-    others(lambda peer: a_copy(peer, peer).wait_recv())
-
     chunk_cols = min(half, 512)
-
-    def columns(step, carry):
-        at = pl.ds(pl.multiple_of(step * chunk_cols, chunk_cols), chunk_cols)
-        spec[:, at] = jnp.dot(recv_a[...], two[:, at], preferred_element_type=f32)
-        return carry
-
-    lax.fori_loop(0, 2 * second // chunk_cols, columns, 0)
+    deep = group * width
+
+    def gather(step, carry):
+        chunk = lax.rem(own_set + sets - 1 - step, sets)
+        for member in range(group):
+            peer = chunk * group + member
+
+            @pl.when(peer != me)
+            def _():
+                a_copy(peer, peer).wait_recv()
+        block = pl.ds(pl.multiple_of(chunk * deep, deep), deep)
+
+        def columns(tile, inner):
+            at = pl.ds(pl.multiple_of(tile * chunk_cols, chunk_cols), chunk_cols)
+            spec[:, at] += jnp.dot(recv_a[:, block], two[block, at], preferred_element_type=f32)
+            return inner
+
+        return lax.fori_loop(0, 2 * second // chunk_cols, columns, carry)
+
+    lax.fori_loop(0, sets, gather, 0)
 
     def power(start):
-        total = jnp.zeros((rows, half), f32)
+        found = jnp.zeros((rows, half), f32)
         for pair in range(pairs):
             for part in (start, start + half):
                 value = spec[pair * rows:(pair + 1) * rows, part:part + half]
-                total = total + value * value
-        return total
+                found = found + value * value
+        return found
 
     far = power(second)
     near_row = lax.broadcasted_iota(jnp.int32, (rows, rows), 0)
@@ -339,15 +359,15 @@
             device_id={"tmpl": peer}, device_id_type=pl.DeviceIdType.MESH)
 
     def filters(step, carry):
-        peer = lax.rem(me + step, devs)
+        peer = lax.rem(own_set + 1 + step // group, sets) * group + lax.rem(step + me, group)
         which = order[peer]
         inside = freq < cutoff[which]
         real, imag = bank[0, which].astype(f32), bank[1, which].astype(f32)
         send_q[peer, :, :half] = jnp.where(inside, white_real * real + white_imag * imag, 0.0).astype(bf16)
         send_q[peer, :, half:] = jnp.where(inside, white_imag * real - white_real * imag, 0.0).astype(bf16)
         weight = jnp.where(inside, (real * real + imag * imag) * inverse, 0.0)
-        total = sum(weight[at:at + 8] for at in range(0, rows, 8))
-        norm_out[peer] = sum(total[:, at:at + 128] for at in range(0, half, 128))
+        folded = sum(weight[at:at + 8] for at in range(0, rows, 8))
+        norm_out[peer] = sum(folded[:, at:at + 128] for at in range(0, half, 128))
 
         @pl.when(peer != me)
         def _():
@@ -355,43 +375,55 @@
             n_copy(peer, me).start()
         return carry
 
-    lax.fori_loop(1, devs + 1, filters, 0)
+    lax.fori_loop(0, devs, filters, 0)
     recv_q[pl.ds(pl.multiple_of(me * rows, rows), rows), :] = send_q[me]
     norm_in[me] = norm_out[me]
     for copy in loads[8:]:
         copy.wait()
 
-    def rows_back(step, carry):
-        chunk = lax.rem(own_set + step, sets)
+    tail = 256
+    tall = group * rows
+
+    def rows_back(step):
+        chunk = lax.rem(own_set + sets - 1 - step, sets)
         for member in range(group):
             peer = chunk * group + member
 
             @pl.when(peer != me)
             def _():
                 q_copy(peer, peer).wait_recv()
-        at = pl.ds(pl.multiple_of(chunk * group * rows, group * rows), group * rows)
-        below = pl.ds(pl.multiple_of(first + chunk * group * rows, group * rows), group * rows)
+        at = pl.ds(pl.multiple_of(chunk * tall, tall), tall)
         wide = jnp.dot(recv_q[at, :], inv[...], preferred_element_type=f32)
         real, imag = wide[:, :second], wide[:, second:]
         cos, sin = ucos[at, :].astype(f32), usin[at, :].astype(f32)
-        lifted[at, :] = (real * cos - imag * sin).astype(bf16)
-        lifted[below, :] = (real * sin + imag * cos).astype(bf16)
-        return carry
-
-    lax.fori_loop(0, sets, rows_back, 0)
+        lifted[:tall, :] = (real * cos - imag * sin).astype(bf16)
+        lifted[tall:, :] = (real * sin + imag * cos).astype(bf16)
+        return chunk
+
+    def back(step, carry):
+        chunk = rows_back(step)
+
+        def cols_back(tile, inner):
+            at = pl.ds(pl.multiple_of(tile * tail, tail), tail)
+            total[:, at] += jnp.dot(last[chunk], lifted[:, at], preferred_element_type=f32)
+            return inner
+
+        return lax.fori_loop(0, second // tail, cols_back, carry)
+
+    lax.fori_loop(0, sets - 1, back, 0)
     others(lambda peer: n_copy(peer, peer).wait_recv())
     norm = jnp.sum(jnp.sum(jnp.sum(norm_in[...], 0), 0, keepdims=True), 1, keepdims=True)
     gain = 1.0 / jnp.sqrt(norm)
-    tail = 256
-
-    def cols_back(step, carry):
-        at = pl.ds(pl.multiple_of(step * tail, tail), tail)
-        field = jnp.dot(last[...], lifted[:, at], preferred_element_type=f32)
+    chunk = rows_back(sets - 1)
+
+    def finish(tile, carry):
+        at = pl.ds(pl.multiple_of(tile * tail, tail), tail)
+        field = total[:, at] + jnp.dot(last[chunk], lifted[:, at], preferred_element_type=f32)
         real, imag = field[:first], field[first:]
         out[0, :, at] = (jnp.sqrt(real * real + imag * imag) * gain).astype(bf16)
         return carry
 
-    lax.fori_loop(0, second // tail, cols_back, 0)
+    lax.fori_loop(0, second // tail, finish, 0)
 
     def drain(peer):
         a_copy(peer, me).wait_send()
@@ -412,12 +444,12 @@
     second = cols * devs
     half = second // 2
     rows = first // devs
-    group = 4
+    group = GROUP
     parts = segs // 2 + 1
     f32, bf16 = jnp.float32, jnp.bfloat16
     consts = [jnp.asarray(part) for part in tables(devs, first, cols)]
     smem = pl.BlockSpec(memory_space=pltpu.SMEM)
-    held = [strain, analysis, bank] + consts
+    held = [strain.transpose(0, 2, 1), analysis.T, bank] + consts
     shapes = [part.shape for part in held]
     for at in (4, 5, 6):
         shapes[at] = shapes[at][1:]
@@ -429,7 +461,7 @@
         in_specs=[smem, smem] + [pl.BlockSpec(memory_space=pl.ANY)] * len(held),
         out_specs=pl.BlockSpec(memory_space=vmem),
         scratch_shapes=[vmem(shape, part.dtype) for shape, part in zip(shapes, held)] + [
-            vmem((first, parts * 2 * cols), bf16),
+            vmem((parts * 2 * cols, first), bf16),
             vmem((devs, parts * rows, 2 * cols), bf16),
             vmem((parts * rows, 2 * second), bf16),
             vmem((parts * rows, 2 * second), f32),
@@ -437,7 +469,7 @@
             vmem((8, half), f32), vmem((8, half), f32),
             vmem((devs, rows, 2 * half), bf16), vmem((first, 2 * half), bf16),
             vmem((devs, 8, 128), f32), vmem((devs, 8, 128), f32),
-            vmem((2 * first, second), bf16),
+            vmem((2 * group * rows, second), bf16), vmem((2 * first, second), f32),
             dma((len(held),)), dma((devs,)), dma((devs,)), dma((2,)), dma((2,)),
             dma((devs,)), dma((devs,)), dma((devs,)), dma((devs,)),
         ],
@@ -449,7 +481,7 @@
 def fits(strain, bank, devs):
     segs, first, cols = strain.shape
     rows = first // devs
-    return (2 * cols == 128 and rows % 16 == 0 and segs % 2 == 0 and devs % 4 == 0
+    return (2 * cols == 128 and rows % 16 == 0 and segs % 2 == 0 and devs % GROUP == 0
             and bank.shape[1] == devs)
 
 

time: 67.1 us -> 62.6 us (0.933)
  the two profiles are of different devices: /device:TPU:15 before, /device:TPU:11 now
where the time goes in v1:
time: 62.6 us; the launch traced here: 62.4 us
  Pallas kernels  60.2 us (96%)
  local copies, waits for them, and re-layouts  2.26 us (4%)
    pallas_call x1, Pallas kernels, fused(): pl.pallas_call(functools.partial(kernel, devs, group), out_shape=jax.Shap...  60.2 us
    unnamed x1, local copies, waits for them, and re-layouts  2.26 us

profile of v1, /device:TPU:11, one launch (start us, length us, event | category | flops | bytes accessed | tf_op | source)
XLA Modules:
  0.0 62.4 jit_solution(3997124668517135868)
XLA Ops:
  0.0 60.2 %shard_map.136 = bf16[1,512,1024]{2,1,0:T(8,128)(2,1)} custom-call(s32[16]{0:T(128)} %cutoff.1, s32[16]{0:T(128)} %order.1, f32[8,64,512]{2,1,0:T(8,128)} %bitcast.2, f32[64,512]{1,0:T(8,128)} %bitcast.3, bf16[2,16,32,512]{3,2,1,0:T(8,128)(2,1)} %bank_h.1, bf16[16,64,512]{2,1,0:T(8,128)(2,1)} %constant.18.clone.one_h, ...), custom_call_target="tpu_custom_call" | custom-call | tf_op jit(solution)/shard_map/pallas_call | solution.py:458
  60.2 2.3 %copy.16 = bf16[1,512,1024]{2,1,0:T(8,128)(2,1)} copy(bf16[1,512,1024]{2,1,0:T(8,128)(2,1)} %shard_map.136) | data formatting | bytes 2097152
